TPU v7x, 32 devices: a whole 2x2x4 slice. The times are simulated.
32 devices in a mesh: groups: 2 (over y), strip: 4 (over z), slab: 2 (over x), sub: 2 (over core).
Axes of the slice: x: 2, y: 2, z: 4, core: 2. Of those that a mesh axis runs over, the one named last changes fastest.
Arguments:
- features: bfloat16 [8, 2, 2, 12, 8, 8, 512], P(('groups', 'strip'), 'sub', 'slab'), parts along dimension 0, may hold values from -6 to 6
- voxel_mask: int32 [8, 2, 2, 12, 8, 8, 8], P(('groups', 'strip'), 'sub', 'slab'), parts along dimension 0, may hold values 0 or 1
- block_pos: int32 [8, 2, 2, 12], P(('groups', 'strip'), 'sub', 'slab'), parts along dimension 0, may hold values from 0 to 16, as said below
- conv_weight: bfloat16 [3, 3, 3, 64, 64], replicated, may hold values from -0.21875 to 0.21875
- conv_gain: float32 [64], replicated, may hold values from 0.25 to 1.75
- conv_bias: float32 [64], replicated, may hold values from -1.2 to 1.2
- height_weight: bfloat16 [2048, 128], P('slab'), may hold values from -0.375 to 0.375
- height_bias: float32 [128], replicated, may hold values from -1.2 to 1.2
- bev_weight: bfloat16 [3, 3, 128, 256], replicated, may hold values from -0.25 to 0.25
- bev_gain: float32 [256], replicated, may hold values from 0.25 to 1.75
- bev_bias: float32 [256], replicated, may hold values from -1.2 to 1.2
- head_weight: bfloat16 [256, 11], replicated, may hold values from -0.5 to 0.5
- head_bias: float32 [11], replicated, may hold values from -2 to 2
Outputs:
- head_maps: float32 [64, 128, 11], P(('groups', 'strip', 'slab'), 'sub'), parts along dimension 0
There are 2 independent parts, one for each index of `groups`. A program takes and returns all parts, laid end to end along the dimension named above; an argument that names none is the same for every part. Nothing has to cross between parts.
Inputs may be any that keep to these rules, and one draw needn't show every extreme that they name: `block_pos`: on each device the live slots name distinct positions below 16; the empty ones hold 16. In every draw some device has all 12 slots live.
All inputs are finite; a program needn't handle non-finite values. No bound on the sum of `voxel_mask` on one device may be relied on, other than what follows from the above.
Results may differ from a plain program's by a relative error of at most 0.0041.
Values may be sent and summed in bfloat16 or wider, within the bound.
A program may use at most 128 MiB of HBM per device.

v0:
```python
import jax
import jax.numpy as jnp
from jax import lax
from jax.sharding import PartitionSpec as P

BY_DEV = 8
BZ_DEV = 2


def extended_2(cells, sides, width):
    for axis, dim in sides:
        count = lax.axis_size(axis)
        ends = count - 1
        head = lax.slice_in_dim(cells, 0, width, axis=dim)
        tail = lax.slice_in_dim(cells, cells.shape[dim] - width, cells.shape[dim], axis=dim)
        cells = jnp.concatenate(
            [
                lax.ppermute(tail, axis, [(i, (i + 1) % count) for i in range(ends)]),
                cells,
                lax.ppermute(head, axis, [((i + 1) % count, i) for i in range(ends)]),
            ],
            axis=dim,
        )
    return cells


def banded_taps(conv_weight, edge_len, chan_count):
    offsets = jnp.arange(edge_len + 2)[:, None] - jnp.arange(edge_len)[None, :]
    selector = (offsets[None, :, :] == jnp.arange(3)[:, None, None]).astype(jnp.bfloat16)
    banded = jnp.einsum(
        "kio,abkcd->abicod", selector, conv_weight, preferred_element_type=jnp.float32
    )
    return banded.reshape(3, 3, (edge_len + 2) * chan_count, edge_len * chan_count).astype(
        jnp.bfloat16
    )


def sweep_taps(windows, banded, rows_x, rows_y):
    totals = jnp.zeros((windows.shape[0] * rows_x * rows_y, banded.shape[3]), jnp.float32)
    for shift_x in range(3):
        for shift_y in range(3):
            sliced = windows[:, shift_x : shift_x + rows_x, shift_y : shift_y + rows_y, :]
            totals = totals + jnp.dot(
                sliced.reshape(-1, windows.shape[3]),
                banded[shift_x, shift_y],
                preferred_element_type=jnp.float32,
            )
    return totals.reshape(windows.shape[0], rows_x, rows_y, banded.shape[3])


def to_region(blocks, places, positions, blocks_y, blocks_z):
    table = jnp.zeros((positions + 1,) + blocks.shape[1:], blocks.dtype).at[places].set(blocks)
    table = table[:positions].reshape((blocks_y, blocks_z) + blocks.shape[1:])
    edge_len = blocks.shape[1]
    return table.transpose(2, 0, 3, 1, 4).reshape(
        edge_len, blocks_y * edge_len, blocks_z * blocks.shape[3]
    )


def on_device(
    features,
    voxel_mask,
    block_pos,
    conv_weight,
    conv_gain,
    conv_bias,
    height_weight,
    height_bias,
    bev_weight,
    bev_gain,
    bev_bias,
    head_weight,
    head_bias,
):
    blocks = features[0, 0, 0]
    edge_len = blocks.shape[1]
    chan_count = blocks.shape[3] // edge_len
    blocks_y = BY_DEV
    blocks_z = BZ_DEV
    positions = blocks_y * blocks_z
    places = block_pos[0, 0, 0]
    live_mask = voxel_mask[0, 0, 0].astype(jnp.bfloat16)
    wide_mask = jnp.broadcast_to(live_mask[..., None], live_mask.shape + (chan_count,)).reshape(
        blocks.shape
    )
    masked = blocks * wide_mask
    region = to_region(masked, places, positions, blocks_y, blocks_z)
    lifted = extended_2(region, (("slab", 2),), chan_count)
    extended = extended_2(lifted, (("strip", 0), ("sub", 1)), 1)
    banded = banded_taps(conv_weight, edge_len, chan_count)
    columns = []
    for z_level in range(blocks_z):
        low_edge = z_level * edge_len * chan_count
        window = extended[None, :, :, low_edge : low_edge + (edge_len + 2) * chan_count]
        columns.append(sweep_taps(window, banded, edge_len, blocks_y * edge_len)[0])
    pre_act = jnp.concatenate(columns, axis=2)
    region_mask = to_region(wide_mask, places, positions, blocks_y, blocks_z)
    gain_wide = jnp.tile(conv_gain, blocks_z * edge_len)
    bias_wide = jnp.tile(conv_bias, blocks_z * edge_len)
    voxel_region = (jax.nn.relu(pre_act * gain_wide + bias_wide) * region_mask).astype(jnp.bfloat16)
    row_share = edge_len // lax.axis_size("slab")
    col_width = voxel_region.shape[1]
    sums_part = jnp.dot(
        voxel_region.reshape(row_share * lax.axis_size("slab") * col_width, -1),
        height_weight,
        preferred_element_type=jnp.float32,
    )
    column_sums = lax.psum_scatter(
        sums_part.reshape(row_share * lax.axis_size("slab"), col_width * height_weight.shape[1]),
        "slab",
        scatter_dimension=0,
        tiled=True,
    ).reshape(row_share * col_width, -1)
    bev = (
        jax.nn.relu(column_sums + height_bias)
        .astype(jnp.bfloat16)
        .reshape(row_share, col_width, -1)
    )
    bev_ext = extended_2(bev, ((("strip", "slab"), 0), ("sub", 1)), 1)
    bev_pre = jnp.zeros((row_share * col_width, bev_weight.shape[3]), jnp.float32)
    for shift_x in range(3):
        for shift_y in range(3):
            sliced = bev_ext[shift_x : shift_x + row_share, shift_y : shift_y + col_width, :]
            bev_pre = bev_pre + jnp.dot(
                sliced.reshape(row_share * col_width, -1),
                bev_weight[shift_x, shift_y],
                preferred_element_type=jnp.float32,
            )
    hidden = jax.nn.relu(bev_pre * bev_gain + bev_bias).astype(jnp.bfloat16)
    head_maps = jnp.dot(hidden, head_weight, preferred_element_type=jnp.float32) + head_bias
    return head_maps.reshape(row_share, col_width, -1)


def solution(mesh):
    in_specs = (
        P(("groups", "strip"), "sub", "slab", None, None, None, None),
        P(("groups", "strip"), "sub", "slab", None, None, None, None),
        P(("groups", "strip"), "sub", "slab", None),
        P(),
        P(),
        P(),
        P("slab", None),
        P(),
        P(),
        P(),
        P(),
        P(),
        P(),
    )
    out_specs = P(("groups", "strip", "slab"), "sub", None)
    return jax.shard_map(
        on_device, mesh=mesh, in_specs=in_specs, out_specs=out_specs, check_vma=False
    )
```

profile of v0, /device:TPU:0, one launch (start us, length us, event | category | flops | bytes accessed | tf_op | source)
XLA Modules:
  0.0 156.1 jit_solution(4793895163359020070)
XLA Ops:
  14.6 4.9 %collective-permute-start = (bf16[8,64,64]{2,1,0:T(8,128)(2,1)S(1)}, bf16[8,64,64]{2,1,0:T(8,128)(2,1)S(1)}, u32[]{:S(2)}, u32[]{:S(2)}) collective-permute-start(bf16[8,64,64]{2,1,0:T(8,128)(2,1)S(1)} %get-tuple-element.14), channel_id=1, source_target_pairs={{0,2},{1,3},{4,6},{5,7},{8,10},{9,11},{12,14},{13,15},{16,18},{17,... | collective-permute-start | bytes 196616 | tf_op jit(solution)/shard_map/ppermute | solution.py:18
  19.5 1.3 collective-permute-start.1
  20.8 1.4 collective-permute-done
  22.2 4.2 %collective-permute-done.1 = bf16[8,64,64]{2,1,0:T(8,128)(2,1)} collective-permute-done((bf16[8,64,64]{2,1,0:T(8,128)(2,1)S(1)}, bf16[8,64,64]{2,1,0:T(8,128)(2,1)}, u32[]{:S(2)}, u32[]{:S(2)}) %collective-permute-start.1) | collective-permute-done | bytes 65568 | tf_op jit(solution)/shard_map/ppermute | solution.py:20
  26.4 2.8 %concatenate.33 = bf16[8,64,1152]{2,1,0:T(8,128)(2,1)S(1)} concatenate(bf16[8,64,64]{2,1,0:T(8,128)(2,1)S(1)} %collective-permute-done, bf16[8,64,1024]{2,1,0:T(8,128)(2,1)S(1)} %reshape.178, bf16[8,64,64]{2,1,0:T(8,128)(2,1)} %collective-permute-done.1), dimensions={2} | concatenate | bytes 2359296 | tf_op jit(solution)/shard_map/concatenate | solution.py:16
  29.9 3.5 %collective-permute-start.2 = (bf16[1,64,1152]{2,1,0:T(8,128)(2,1)}, bf16[1,64,1152]{2,1,0:T(8,128)(2,1)S(1)}, u32[]{:S(2)}, u32[]{:S(2)}) collective-permute-start(bf16[1,64,1152]{2,1,0:T(8,128)(2,1)} %get-tuple-element.11), channel_id=1, source_target_pairs={{0,4},{4,8},{8,12},{1,5},{5,9},{9,13},{2,6},{6,10},{10,14},{3,7},{... | collective-permute-start | bytes 442376 | tf_op jit(solution)/shard_map/ppermute | solution.py:18
  33.4 1.3 collective-permute-start.3
  34.7 9.8 %convert_bitcast_fusion = bf16[3,3,10,64,8,64]{5,2,3,1,0,4:T(8,128)(2,1)} fusion(bf16[3,3,3,64,64]{4,3,2,1,0:T(8,128)(2,1)} %param.16, s32[10,8]{0,1:T(8,128)S(1)} %iota_subtract_fusion), kind=kOutput, calls=%fused_computation.2 | convolution fusion | flops 20644080 | bytes 6119744 | tf_op jit(solution)/shard_map/kio,abkcd->abicod/dot_general | solution.py:30
  45.8 1.5 pad_maximum_fusion.6
  47.3 1.9 %collective-permute-start.4 = (bf16[10,1,1152]{2,1,0:T(2,128)(2,1)}, bf16[10,1,1152]{2,1,0:T(2,128)(2,1)}, u32[]{:S(2)}, u32[]{:S(2)}) collective-permute-start(bf16[10,1,1152]{2,1,0:T(2,128)(2,1)} %get-tuple-element.9), channel_id=1, source_target_pairs={{0,1},{2,3},{4,5},{6,7},{8,9},{10,11},{12,13},{14,15},{16,17},{18,... | collective-permute-start | bytes 69128 | tf_op jit(solution)/shard_map/ppermute | solution.py:18
  49.2 1.5 collective-permute-start.5
  51.0 15.2 %copy.28 = bf16[3,3,10,64,8,64]{5,4,3,2,1,0:T(8,128)(2,1)} copy(bf16[3,3,10,64,8,64]{5,2,3,1,0,4:T(8,128)(2,1)} %convert_bitcast_fusion) | data formatting | bytes 11796480 | tf_op jit(solution)/shard_map/convert_element_type | solution.py:33
  66.2 16.3 %convert_element_type.55 = bf16[3,3,640,512]{3,2,1,0:T(8,128)(2,1)} reshape(bf16[3,3,10,64,8,64]{5,4,3,2,1,0:T(8,128)(2,1)} %copy.28) | data formatting | bytes 11796480 | tf_op jit(solution)/shard_map/convert_element_type | solution.py:33
  82.5 1.9 %copy.29 = f32[8,8,8,2,512]{4,3,2,1,0:T(2,128)S(1)} copy(f32[8,8,8,2,512]{4,2,0,3,1:T(8,128)S(1)} %convert_bitcast_fusion.1) | data formatting | bytes 4194304 | tf_op jit(solution)/shard_map/convert_element_type | solution.py:100
  84.5 1.8 %copy.32 = f32[64,8,2,512]{3,1,2,0:T(8,128)} copy(f32[64,8,2,512]{3,2,1,0:T(2,128)S(1)} %bitcast.173) | data formatting | bytes 4194304
  86.3 1.9 %copy.30 = f32[512,1024]{0,1:T(8,128)S(1)} copy(f32[512,1024]{1,0:T(8,128)} %bitcast.174) | data formatting | bytes 4194304 | tf_op jit(solution)/shard_map/convert_element_type | solution.py:100
  88.4 1.5 pad_maximum_fusion
  90.1 3.1 %fusion.53 = (bf16[1,8,64,640]{3,2,1,0:T(8,128)(2,1)S(1)}, bf16[1,8,64,640]{3,2,1,0:T(8,128)(2,1)S(1)}, bf16[1,8,64,640]{3,2,1,0:T(8,128)(2,1)S(1)}, bf16[1,8,64...) fusion(bf16[1,10,66,640]{3,2,1,0:T(8,128)(2,1)S(1)} %get-tuple-, ...), kind=kLoop, calls=%fused_computation.111 | loop fusion | bytes 23592960 | tf_op jit(solution)/shard_map/slice | solution.py:42
  107.5 25.3 %all-reduce.3.cloned.1.call-done = f32[8,8192]{1,0:T(8,128)} async-done(((f32[8,8192]{1,0:T(8,128)}), f32[8,8192]{1,0:T(8,128)}) %all-reduce.3.cloned.1.call-update) | async-done | bytes 262160
  134.0 2.2 %collective-permute-start.6 = (bf16[1,64,128]{2,1,0:T(8,128)(2,1)S(1)}, bf16[1,64,128]{2,1,0:T(8,128)(2,1)S(1)}, u32[]{:S(2)}, u32[]{:S(2)}) collective-permute-start(bf16[1,64,128]{2,1,0:T(8,128)(2,1)S(1)} %get-tuple-element.45), channel_id=1, source_target_pairs={{0,2},{2,4},{4,6},{6,8},{8,10},{10,12},{12,14},{1,3},{3,5},{5,7},{... | collective-permute-start | bytes 49160 | tf_op jit(solution)/shard_map/ppermute | solution.py:18
  136.2 1.3 collective-permute-start.7
  137.6 4.9 %collective-permute-done.7 = bf16[1,64,128]{2,1,0:T(8,128)(2,1)S(1)} collective-permute-done((bf16[1,64,128]{2,1,0:T(8,128)(2,1)S(1)}, bf16[1,64,128]{2,1,0:T(8,128)(2,1)S(1)}, u32[]{:S(2)}, u32[]{:S(2)}) %collective-permute-start.7) | collective-permute-done | bytes 16416 | tf_op jit(solution)/shard_map/ppermute | solution.py:20
  143.8 1.3 collective-permute-start.9
  145.3 1.5 collective-permute-done.9
  (104 shorter events, 29.0 us)
Async XLA Ops:
  6.5 98.0 %copy-start = (bf16[1024,128]{1,0:T(8,128)(2,1)S(1)}, bf16[1024,128]{1,0:T(8,128)(2,1)}, u32[]{:S(2)}) copy-start(bf16[1024,128]{1,0:T(8,128)(2,1)} %param.19) | copy-start | bytes 786436
  6.5 3.6 %copy-start.10 = (s32[1,1,1,12]{3,2,1,0:T(1,128)S(1)}, s32[1,1,1,12]{3,2,1,0:T(1,128)}, u32[]{:S(2)}) copy-start(s32[1,1,1,12]{3,2,1,0:T(1,128)} %param.15) | copy-start | bytes 148
  6.5 126.3 %all-reduce.3.cloned.1.call-start = ((), (), s32[]{:S(2)}) async-start(), calls=%async_computation | async-start | bytes 524288
  14.6 7.6 %collective-permute-start = (bf16[8,64,64]{2,1,0:T(8,128)(2,1)S(1)}, bf16[8,64,64]{2,1,0:T(8,128)(2,1)S(1)}, u32[]{:S(2)}, u32[]{:S(2)}) collective-permute-start(bf16[8,64,64]{2,1,0:T(8,128)(2,1)S(1)} %get-tuple-element.14), channel_id=1, source_target_pairs={{0,2},{1,3},{4,6},{5,7},{8,10},{9,11},{12,14},{13,15},{16,18},{17,... | collective-permute-start | bytes 196616 | tf_op jit(solution)/shard_map/ppermute | solution.py:18
  19.5 7.0 %collective-permute-start.1 = (bf16[8,64,64]{2,1,0:T(8,128)(2,1)S(1)}, bf16[8,64,64]{2,1,0:T(8,128)(2,1)}, u32[]{:S(2)}, u32[]{:S(2)}) collective-permute-start(bf16[8,64,64]{2,1,0:T(8,128)(2,1)S(1)} %get-tuple-element.13), channel_id=1, source_target_pairs={{2,0},{3,1},{6,4},{7,5},{10,8},{11,9},{14,12},{15,13},{18,16},{19,... | collective-permute-start | bytes 196616 | tf_op jit(solution)/shard_map/ppermute | solution.py:20
  29.9 15.9 %collective-permute-start.2 = (bf16[1,64,1152]{2,1,0:T(8,128)(2,1)}, bf16[1,64,1152]{2,1,0:T(8,128)(2,1)S(1)}, u32[]{:S(2)}, u32[]{:S(2)}) collective-permute-start(bf16[1,64,1152]{2,1,0:T(8,128)(2,1)} %get-tuple-element.11), channel_id=1, source_target_pairs={{0,4},{4,8},{8,12},{1,5},{5,9},{9,13},{2,6},{6,10},{10,14},{3,7},{... | collective-permute-start | bytes 442376 | tf_op jit(solution)/shard_map/ppermute | solution.py:18
  33.4 12.4 %collective-permute-start.3 = (bf16[1,64,1152]{2,1,0:T(8,128)(2,1)}, bf16[1,64,1152]{2,1,0:T(8,128)(2,1)}, u32[]{:S(2)}, u32[]{:S(2)}) collective-permute-start(bf16[1,64,1152]{2,1,0:T(8,128)(2,1)} %get-tuple-element.12), channel_id=1, source_target_pairs={{4,0},{8,4},{12,8},{5,1},{9,5},{13,9},{6,2},{10,6},{14,10},{7,3},{... | collective-permute-start | bytes 442376 | tf_op jit(solution)/shard_map/ppermute | solution.py:20
  45.8 4.9 %copy-start.1 = (bf16[1,64,1152]{2,1,0:T(8,128)(2,1)}, bf16[1,64,1152]{2,1,0:T(8,128)(2,1)S(1)}, u32[]{:S(2)}) copy-start(bf16[1,64,1152]{2,1,0:T(8,128)(2,1)S(1)} %collective-permute-done.2) | copy-start | bytes 442372
  47.3 41.1 %collective-permute-start.4 = (bf16[10,1,1152]{2,1,0:T(2,128)(2,1)}, bf16[10,1,1152]{2,1,0:T(2,128)(2,1)}, u32[]{:S(2)}, u32[]{:S(2)}) collective-permute-start(bf16[10,1,1152]{2,1,0:T(2,128)(2,1)} %get-tuple-element.9), channel_id=1, source_target_pairs={{0,1},{2,3},{4,5},{6,7},{8,9},{10,11},{12,13},{14,15},{16,17},{18,... | collective-permute-start | bytes 69128 | tf_op jit(solution)/shard_map/ppermute | solution.py:18
  49.2 39.2 %collective-permute-start.5 = (bf16[10,1,1152]{2,1,0:T(2,128)(2,1)}, bf16[10,1,1152]{2,1,0:T(2,128)(2,1)}, u32[]{:S(2)}, u32[]{:S(2)}) collective-permute-start(bf16[10,1,1152]{2,1,0:T(2,128)(2,1)} %get-tuple-element.10), channel_id=1, source_target_pairs={{1,0},{3,2},{5,4},{7,6},{9,8},{11,10},{13,12},{15,14},{17,16},{19,... | collective-permute-start | bytes 69128 | tf_op jit(solution)/shard_map/ppermute | solution.py:20
  84.5 3.8 %copy-start.8 = (f32[64]{0:T(128)S(1)}, f32[64]{0:T(128)}, u32[]{:S(2)}) copy-start(f32[64]{0:T(128)} %param.18) | copy-start | bytes 772
  84.5 3.8 %copy-start.9 = (f32[64]{0:T(128)S(1)}, f32[64]{0:T(128)}, u32[]{:S(2)}) copy-start(f32[64]{0:T(128)} %param.17) | copy-start | bytes 772
  89.9 3.3 %slice-start = ((s8[5898240]{0:T(1024)(128)(4,1)}), s8[4194304]{0:T(1024)(128)(4,1)S(1)}, s32[]{:S(2)}) async-start(s8[5898240]{0:T(1024)(128)(4,1)} %bitcast.171), calls=%async_computation.1 | async-start | bytes 8388608
  90.1 3.2 %slice-start.1 = ((s8[5898240]{0:T(1024)(128)(4,1)}), s8[1703936]{0:T(1024)(128)(4,1)S(1)}, s32[]{:S(2)}) async-start(s8[5898240]{0:T(1024)(128)(4,1)} %bitcast.171), calls=%async_computation.2 | async-start | bytes 3407872
  104.5 3.0 %copy-start.4 = (f32[128]{0:T(128)S(1)}, f32[128]{0:T(128)}, u32[]{:S(2)}) copy-start(f32[128]{0:T(128)} %param.20) | copy-start | bytes 1540
  104.6 40.6 %copy-start.2 = (bf16[3,3,128,256]{3,2,1,0:T(8,128)(2,1)S(1)}, bf16[3,3,128,256]{3,2,1,0:T(8,128)(2,1)}, u32[]{:S(2)}) copy-start(bf16[3,3,128,256]{3,2,1,0:T(8,128)(2,1)} %param.21) | copy-start | bytes 1769476
  134.0 14.3 %copy-start.3 = (bf16[256,11]{0,1:T(8,128)(2,1)S(1)}, bf16[256,11]{0,1:T(8,128)(2,1)}, u32[]{:S(2)}) copy-start(bf16[256,11]{0,1:T(8,128)(2,1)} %param.24) | copy-start | bytes 16900
  134.0 14.3 %copy-start.5 = (f32[256]{0:T(256)S(1)}, f32[256]{0:T(256)}, u32[]{:S(2)}) copy-start(f32[256]{0:T(256)} %param.23) | copy-start | bytes 3076
  134.0 14.3 %copy-start.6 = (f32[256]{0:T(256)S(1)}, f32[256]{0:T(256)}, u32[]{:S(2)}) copy-start(f32[256]{0:T(256)} %param.22) | copy-start | bytes 3076
  134.0 14.3 %copy-start.7 = (f32[11]{0:T(128)S(1)}, f32[11]{0:T(128)}, u32[]{:S(2)}) copy-start(f32[11]{0:T(128)} %param.25) | copy-start | bytes 136
  134.0 3.6 %collective-permute-start.6 = (bf16[1,64,128]{2,1,0:T(8,128)(2,1)S(1)}, bf16[1,64,128]{2,1,0:T(8,128)(2,1)S(1)}, u32[]{:S(2)}, u32[]{:S(2)}) collective-permute-start(bf16[1,64,128]{2,1,0:T(8,128)(2,1)S(1)} %get-tuple-element.45), channel_id=1, source_target_pairs={{0,2},{2,4},{4,6},{6,8},{8,10},{10,12},{12,14},{1,3},{3,5},{5,7},{... | collective-permute-start | bytes 49160 | tf_op jit(solution)/shard_map/ppermute | solution.py:18
  136.2 6.3 %collective-permute-start.7 = (bf16[1,64,128]{2,1,0:T(8,128)(2,1)S(1)}, bf16[1,64,128]{2,1,0:T(8,128)(2,1)S(1)}, u32[]{:S(2)}, u32[]{:S(2)}) collective-permute-start(bf16[1,64,128]{2,1,0:T(8,128)(2,1)S(1)} %get-tuple-element.46), channel_id=1, source_target_pairs={{2,0},{4,2},{6,4},{8,6},{10,8},{12,10},{14,12},{3,1},{5,3},{7,5},{... | collective-permute-start | bytes 49160 | tf_op jit(solution)/shard_map/ppermute | solution.py:20
  142.5 2.8 %collective-permute-start.8 = (bf16[6,1,128]{2,1,0:T(2,128)(2,1)S(1)}, bf16[6,1,128]{2,1,0:T(2,128)(2,1)S(1)}, u32[]{:S(2)}, u32[]{:S(2)}) collective-permute-start(bf16[6,1,128]{2,1,0:T(2,128)(2,1)S(1)} %get-tuple-element.41), channel_id=1, source_target_pairs={{0,1},{2,3},{4,5},{6,7},{8,9},{10,11},{12,13},{14,15},{16,17},{18,... | collective-permute-start | bytes 4616 | tf_op jit(solution)/shard_map/ppermute | solution.py:18
  143.8 3.1 %collective-permute-start.9 = (bf16[6,1,128]{2,1,0:T(2,128)(2,1)S(1)}, bf16[6,1,128]{2,1,0:T(2,128)(2,1)S(1)}, u32[]{:S(2)}, u32[]{:S(2)}) collective-permute-start(bf16[6,1,128]{2,1,0:T(2,128)(2,1)S(1)} %get-tuple-element.42), channel_id=1, source_target_pairs={{1,0},{3,2},{5,4},{7,6},{9,8},{11,10},{13,12},{15,14},{17,16},{19,... | collective-permute-start | bytes 4616 | tf_op jit(solution)/shard_map/ppermute | solution.py:20
  (1 other events, 1.7 us)
Sparse Core Ops, SparseCore 0:
  106.4 26.4 all-reduce.2
where the time goes:
time: 158 us; the launch traced here: 156 us
  local copies, waits for them, and re-layouts  53.4 us (34%)
  waiting for transfers between devices  37.4 us (24%)
  matrix products  23.5 us (15%)
  starting transfers between devices  20.3 us (13%)
  between operations  14.8 us (9%)
  other arithmetic  6.64 us (4%)
    convert_element_type x2, local copies, waits for them, and re-layouts, banded_taps(): banded.reshape(3, 3, (edge_len + 2) * chan_count, edge_len * chan_count)  31.5 us
    unnamed x2, waiting for transfers between devices  25.3 us
    ppermute x5, starting transfers between devices, extended_2(): lax.ppermute(tail, axis, [(i, (i + 1) % count) for i in range(ends)])  13.7 us
    dot_general x18, matrix products, sweep_taps(): jnp.dot(sliced.reshape(-1, windows.shape[3]), banded[shift_x, shift_y], p...  11.1 us
    ppermute x5, waiting for transfers between devices, extended_2(): lax.ppermute(head, axis, [((i + 1) % count, i) for i in range(ends)])  10.7 us
    dot_general x1, matrix products, banded_taps(): jnp.einsum('kio,abkcd->abicod', selector, conv_weight, preferred_element_...  9.84 us
    ppermute x5, starting transfers between devices, extended_2(): lax.ppermute(head, axis, [((i + 1) % count, i) for i in range(ends)])  6.63 us
    convert_element_type x2, local copies, waits for them, and re-layouts, on_device(): jax.nn.relu(pre_act * gain_wide + bias_wide) * region_mask  3.83 us
  transfers between devices with their start and end apart: 11, of which 5 were waited for; matrix products, arithmetic and copies ran while one was open for 32% of the time, Pallas kernels for 0%

commit v1 on v0

v1 whole, which is shorter than its diff:
```python
import jax
import jax.numpy as jnp
from jax import lax
from jax.experimental import pallas as pl
from jax.experimental.pallas import tpu as pltpu
from jax.sharding import PartitionSpec as P

BY_DEV = 8
BZ_DEV = 2
MESH = pl.DeviceIdType.MESH
F32 = jnp.float32
BF16 = jnp.bfloat16

DIRS = [(a, b) for a in (-1, 0, 1) for b in (-1, 0, 1) if (a, b) != (0, 0)]


def body(
    sizes,
    pos_ref,
    feat_ref,
    mask_ref,
    cw_ref,
    gain_ref,
    bias_ref,
    hw_ref,
    hb_ref,
    bw_ref,
    bgain_ref,
    bbias_ref,
    head_ref,
    headb_ref,
    out_ref,
    xbuf,
    xm,
    xp,
    ybuf,
    wide,
    mbuf,
    band,
    part,
    edge,
    rbuf,
    cbuf,
    hcol,
    bexp,
    face_send,
    face_recv,
    y_send,
    y_recv,
    sum_send,
    sum_recv,
    col_send,
    col_recv,
):
    n_strip, n_slab, n_sub = sizes
    share = 8 // n_slab
    s = lax.axis_index("strip")
    l = lax.axis_index("slab")
    u = lax.axis_index("sub")

    barrier = pltpu.get_barrier_semaphore()
    for a in (-1, 0, 1):

        @pl.when((s + a >= 0) & (s + a < n_strip))
        def _():
            for dl in range(n_slab):
                for du in range(n_sub):
                    if a == 0 and dl == 0 and du == 0:
                        continue
                    pl.semaphore_signal(
                        barrier,
                        inc=1,
                        device_id={
                            "strip": s + a,
                            "slab": lax.rem(l + dl, n_slab),
                            "sub": lax.rem(u + du, n_sub),
                        },
                        device_id_type=MESH,
                    )

    chan_of = lax.broadcasted_iota(jnp.int32, (8, 512), 1) // 64
    level_of = lax.broadcasted_iota(jnp.int32, (8, 512), 0)
    spread = (chan_of == level_of).astype(F32).astype(BF16)
    wide[...] = jnp.dot(
        mask_ref[...].reshape(12 * 64, 8).astype(F32).astype(BF16),
        spread,
        preferred_element_type=F32,
    ).reshape(12, 64, 512)

    def slot_at(place):
        slot = jnp.int32(0)
        live = jnp.int32(0)
        for t in range(12):
            hit = pos_ref[t] == place
            slot = jnp.where(hit, t, slot)
            live = jnp.where(hit, 1, live)
        return slot, live.astype(F32)

    for pz in range(BZ_DEV):
        for pair in range(BY_DEV // 2):
            masks, blocks = [], []
            for half in range(2):
                slot, live = slot_at((2 * pair + half) * BZ_DEV + pz)
                mask = wide[slot] * live
                masks.append(mask.reshape(8, 8, 512))
                blocks.append((feat_ref[slot].astype(F32) * mask).reshape(8, 8, 512))
            rows = pl.ds(16 * pair, 16)
            mbuf[:, rows, pl.ds(512 * pz, 512)] = jnp.concatenate(masks, axis=1).astype(BF16)
            xbuf[pl.ds(1, 8), rows, pl.ds(128 + 512 * pz, 512)] = jnp.concatenate(
                blocks, axis=1
            ).astype(BF16)

    @pl.when(s == 0)
    def _():
        xbuf[0] = jnp.zeros((64, 1280), BF16)

    @pl.when(s == n_strip - 1)
    def _():
        xbuf[9] = jnp.zeros((64, 1280), BF16)

    for edge_row, at_edge in ((0, s > 0), (9, s < n_strip - 1)):

        @pl.when(at_edge & (l == 0))
        def _():
            xbuf[edge_row, :, pl.ds(0, 128)] = jnp.zeros((64, 128), BF16)

        @pl.when(at_edge & (l == n_slab - 1))
        def _():
            xbuf[edge_row, :, pl.ds(1152, 128)] = jnp.zeros((64, 128), BF16)

    @pl.when(l == 0)
    def _():
        xbuf[pl.ds(1, 8), :, pl.ds(0, 128)] = jnp.zeros((8, 64, 128), BF16)

    @pl.when(l == n_slab - 1)
    def _():
        xbuf[pl.ds(1, 8), :, pl.ds(1152, 128)] = jnp.zeros((8, 64, 128), BF16)

    @pl.when(u == 0)
    def _():
        ybuf[0] = jnp.zeros((10, 16, 1280), BF16)

    @pl.when(u == n_sub - 1)
    def _():
        ybuf[1] = jnp.zeros((10, 16, 1280), BF16)

    strips_near = (s > 0).astype(jnp.int32) + (s < n_strip - 1).astype(jnp.int32) + 1
    pl.semaphore_wait(barrier, strips_near * (n_slab * n_sub) - 1)

    def exists(a, b):
        return (s + a >= 0) & (s + a < n_strip) & (l + b >= 0) & (l + b < n_slab)

    def face_copy(at):
        a, b = DIRS[at]
        src_x, dst_x = {-1: ((1, 1), (9, 1)), 0: ((1, 8), (1, 8)), 1: ((8, 1), (0, 1))}[a]
        src_z, dst_z = {
            -1: ((128, 128), (1152, 128)),
            0: ((128, 1024), (128, 1024)),
            1: ((1024, 128), (0, 128)),
        }[b]
        return pltpu.make_async_remote_copy(
            src_ref=xbuf.at[pl.ds(*src_x), :, pl.ds(*src_z)],
            dst_ref=xbuf.at[pl.ds(*dst_x), :, pl.ds(*dst_z)],
            send_sem=face_send.at[at],
            recv_sem=face_recv.at[at],
            device_id={"strip": s + a, "slab": l + b},
            device_id_type=MESH,
        )

    for at, (a, b) in enumerate(DIRS):

        @pl.when(exists(a, b))
        def _():
            face_copy(at).start()

    def make_band(tap, carry):
        blank = jnp.zeros((64, 64), BF16)
        taps = [cw_ref[3 * tap + k] for k in range(3)]
        for e in range(8):
            cols = [taps[e - o - 1] if 0 <= e - o - 1 <= 2 else blank for o in range(4)]
            band[tap, pl.ds(64 * e, 64), :] = jnp.concatenate(cols, axis=1)
        return carry

    lax.fori_loop(0, 9, make_band, 0)

    for at, (a, b) in enumerate(DIRS):

        @pl.when(exists(-a, -b))
        def _():
            face_copy(at).wait_recv()

    def y_copy(side):
        start = 48 if side == 0 else 0
        return pltpu.make_async_remote_copy(
            src_ref=xbuf.at[:, pl.ds(start, 16), :],
            dst_ref=ybuf.at[side],
            send_sem=y_send.at[side],
            recv_sem=y_recv.at[side],
            device_id={"sub": u + 1 if side == 0 else u - 1},
            device_id_type=MESH,
        )

    @pl.when(u < n_sub - 1)
    def _():
        y_copy(0).start()

    @pl.when(u > 0)
    def _():
        y_copy(1).start()

    @pl.when(u > 0)
    def _():
        y_copy(0).wait_recv()

    @pl.when(u < n_sub - 1)
    def _():
        y_copy(1).wait_recv()

    def shift_rows(x, carry):
        rows = xbuf[x].astype(F32)
        row_at = lax.broadcasted_iota(jnp.int32, rows.shape, 0)
        before = ybuf[0, x].astype(F32)[15:16]
        after = ybuf[1, x].astype(F32)[0:1]
        xm[x] = jnp.where(row_at == 0, before, pltpu.roll(rows, 1, 0)).astype(BF16)
        xp[x] = jnp.where(row_at == 63, after, pltpu.roll(rows, 63, 0)).astype(BF16)
        return carry

    lax.fori_loop(0, 10, shift_rows, 0)

    gain4 = jnp.concatenate([gain_ref[...]] * 4, axis=1)
    bias4 = jnp.concatenate([bias_ref[...]] * 4, axis=1)
    part[...] = jnp.zeros_like(part)

    def conv_group(j, carry):
        low = pl.multiple_of(256 * j, 256)
        acc = jnp.zeros((512, 256), F32)
        for dx in range(3):
            for dy, source in enumerate((xm, xbuf, xp)):
                window = source[pl.ds(dx, 8), :, pl.ds(low, 512)].reshape(512, 512)
                acc = acc + jnp.dot(window, band[3 * dx + dy], preferred_element_type=F32)
        mask = mbuf[:, :, pl.ds(low, 256)].reshape(512, 256).astype(F32)
        voxels = (jnp.maximum(acc * gain4 + bias4, 0.0) * mask).astype(BF16)
        sums = jnp.dot(voxels, hw_ref[pl.ds(low, 256), :], preferred_element_type=F32)
        part[...] += sums.reshape(8, 64, 128)
        return carry

    lax.fori_loop(0, 4, conv_group, 0)

    edge[0] = part[:, 56:64, :][:, 7, :]
    edge[1] = part[:, 0:8, :][:, 0, :]

    def row_copy(target, rows, at_row, a, sem, source):
        return pltpu.make_async_remote_copy(
            src_ref=part.at[pl.ds(rows[0], rows[1])],
            dst_ref=rbuf.at[source, pl.ds(at_row, rows[1])],
            send_sem=sum_send.at[sem],
            recv_sem=sum_recv.at[source + n_slab * (a + 1)],
            device_id={"strip": s + a, "slab": target},
            device_id_type=MESH,
        )

    def slab_copy(target, source):
        low = max(0, target * share - 1)
        high = min(8, target * share + share + 1)
        return row_copy(target, (low, high - low), low - (target * share - 1), 0, target, source)

    def up_copy(source):
        return row_copy(0, (7, 1), 0, 1, n_slab, source)

    def down_copy(source):
        return row_copy(n_slab - 1, (0, 1), share + 1, -1, n_slab + 1, source)

    def col_copy(side, a, target, source):
        return pltpu.make_async_remote_copy(
            src_ref=edge.at[side],
            dst_ref=cbuf.at[side, source, pl.ds(8 * (1 - a), 8)],
            send_sem=col_send.at[side, a + 1, target],
            recv_sem=col_recv.at[side, a + 1, source],
            device_id={
                "strip": s + a,
                "slab": target,
                "sub": u + 1 if side == 0 else u - 1,
            },
            device_id_type=MESH,
        )

    has_up = s < n_strip - 1
    has_down = s > 0
    sub_to = (u < n_sub - 1, u > 0)
    sub_from = (u > 0, u < n_sub - 1)
    for t in range(n_slab):

        @pl.when(l != t)
        def _():
            slab_copy(t, l).start()

    @pl.when(has_up)
    def _():
        up_copy(l).start()

    @pl.when(has_down)
    def _():
        down_copy(l).start()

    for side in range(2):

        @pl.when(sub_to[side])
        def _():
            for t in range(n_slab):
                col_copy(side, 0, t, l).start()

        @pl.when(sub_to[side] & has_up)
        def _():
            col_copy(side, 1, 0, l).start()

        @pl.when(sub_to[side] & has_down)
        def _():
            col_copy(side, -1, n_slab - 1, l).start()

    for t in range(n_slab):

        @pl.when(l == t)
        def _():
            low = max(0, t * share - 1)
            high = min(8, t * share + share + 1)
            rbuf[t, pl.ds(low - (t * share - 1), high - low)] = part[pl.ds(low, high - low)]
            for source in range(n_slab):
                if source != t:
                    slab_copy(t, source).wait_recv()

    @pl.when((l == 0) & has_down)
    def _():
        for source in range(n_slab):
            up_copy(source).wait_recv()

    @pl.when((l == 0) & (s == 0))
    def _():
        rbuf[:, pl.ds(0, 1)] = jnp.zeros((n_slab, 1, 64, 128), F32)

    @pl.when((l == n_slab - 1) & has_up)
    def _():
        for source in range(n_slab):
            down_copy(source).wait_recv()

    @pl.when((l == n_slab - 1) & (s == n_strip - 1))
    def _():
        rbuf[:, pl.ds(share + 1, 1)] = jnp.zeros((n_slab, 1, 64, 128), F32)

    for side in range(2):

        @pl.when(sub_from[side])
        def _():
            for source in range(n_slab):
                col_copy(side, 0, 0, source).wait_recv()

        @pl.when(sub_from[side] & (l == 0) & has_down)
        def _():
            for source in range(n_slab):
                col_copy(side, 1, 0, source).wait_recv()

        @pl.when(sub_from[side] & (l == n_slab - 1) & has_up)
        def _():
            for source in range(n_slab):
                col_copy(side, -1, 0, source).wait_recv()

        @pl.when(jnp.logical_not(sub_from[side]))
        def _():
            cbuf[side] = jnp.zeros((n_slab, 24, 128), F32)

        @pl.when(sub_from[side] & jnp.logical_not((l == 0) & has_down))
        def _():
            cbuf[side, :, pl.ds(0, 8)] = jnp.zeros((n_slab, 8, 128), F32)

        @pl.when(sub_from[side] & jnp.logical_not((l == n_slab - 1) & has_up))
        def _():
            cbuf[side, :, pl.ds(16, 8)] = jnp.zeros((n_slab, 8, 128), F32)

    hb = hb_ref[...]
    first_x = s * 8 + l * share - 1

    col_x = lax.broadcasted_iota(jnp.int32, (24, 128), 0) + (s * 8 - 8)
    for side in range(2):
        col = cbuf[side, 0]
        for source in range(1, n_slab):
            col = col + cbuf[side, source]
        inside = (col_x >= 0) & (col_x < 8 * n_strip) & sub_from[side]
        hcol[side] = jnp.where(inside, jnp.maximum(col + hb, 0.0), 0.0)

    for i in range(share + 2):
        total = rbuf[0, i]
        for source in range(1, n_slab):
            total = total + rbuf[source, i]
        total = jnp.maximum(total + hb, 0.0)
        if i == 0 or i == share + 1:
            row_ok = (first_x + i >= 0) & (first_x + i < 8 * n_strip)
            total = jnp.where(row_ok, total, 0.0)
        row_at = lax.broadcasted_iota(jnp.int32, total.shape, 0)
        before = hcol[0, pl.ds(7 + l * share + i, 1), :]
        after = hcol[1, pl.ds(7 + l * share + i, 1), :]
        bexp[i, :, pl.ds(0, 128)] = jnp.where(row_at == 0, before, pltpu.roll(total, 1, 0)).astype(
            BF16
        )
        bexp[i, :, pl.ds(128, 128)] = total.astype(BF16)
        bexp[i, :, pl.ds(256, 128)] = jnp.where(row_at == 63, after, pltpu.roll(total, 63, 0)).astype(
            BF16
        )

    pre = jnp.zeros((share * 64, bw_ref.shape[2]), F32)
    for dx in range(3):
        pre = pre + jnp.dot(
            bexp[pl.ds(dx, share)].reshape(share * 64, 384), bw_ref[dx], preferred_element_type=F32
        )
    hidden = jnp.maximum(pre * bgain_ref[...] + bbias_ref[...], 0.0).astype(BF16)
    out_ref[...] = jnp.dot(hidden, head_ref[...], preferred_element_type=F32) + headb_ref[...]

    for at, (a, b) in enumerate(DIRS):

        @pl.when(exists(a, b))
        def _():
            face_copy(at).wait_send()

    for side in range(2):

        @pl.when(sub_to[side])
        def _():
            y_copy(side).wait_send()
            for t in range(n_slab):
                col_copy(side, 0, t, l).wait_send()

        @pl.when(sub_to[side] & has_up)
        def _():
            col_copy(side, 1, 0, l).wait_send()

        @pl.when(sub_to[side] & has_down)
        def _():
            col_copy(side, -1, n_slab - 1, l).wait_send()

    for t in range(n_slab):

        @pl.when(l != t)
        def _():
            slab_copy(t, l).wait_send()

    @pl.when(has_up)
    def _():
        up_copy(l).wait_send()

    @pl.when(has_down)
    def _():
        down_copy(l).wait_send()


def solution(mesh):
    n_strip, n_slab, n_sub = mesh.shape["strip"], mesh.shape["slab"], mesh.shape["sub"]
    share = 8 // n_slab

    def on_device(
        features,
        voxel_mask,
        block_pos,
        conv_weight,
        conv_gain,
        conv_bias,
        height_weight,
        height_bias,
        bev_weight,
        bev_gain,
        bev_bias,
        head_weight,
        head_bias,
    ):
        heads = head_weight.shape[1]
        chan_out = bev_weight.shape[3]
        vmem = pl.BlockSpec(memory_space=pltpu.VMEM)
        out = pl.pallas_call(
            lambda *refs: body((n_strip, n_slab, n_sub), *refs),
            out_shape=jax.ShapeDtypeStruct((share * 64, heads), F32),
            in_specs=[pl.BlockSpec(memory_space=pltpu.SMEM)] + [vmem] * 12,
            out_specs=vmem,
            scratch_shapes=[
                pltpu.VMEM((10, 64, 1280), BF16),
                pltpu.VMEM((10, 64, 1280), BF16),
                pltpu.VMEM((10, 64, 1280), BF16),
                pltpu.VMEM((2, 10, 16, 1280), BF16),
                pltpu.VMEM((12, 64, 512), F32),
                pltpu.VMEM((8, 64, 1024), BF16),
                pltpu.VMEM((9, 512, 256), BF16),
                pltpu.VMEM((8, 64, 128), F32),
                pltpu.VMEM((2, 8, 128), F32),
                pltpu.VMEM((n_slab, share + 2, 64, 128), F32),
                pltpu.VMEM((2, n_slab, 24, 128), F32),
                pltpu.VMEM((2, 24, 128), F32),
                pltpu.VMEM((share + 2, 64, 384), BF16),
                pltpu.SemaphoreType.DMA((8,)),
                pltpu.SemaphoreType.DMA((8,)),
                pltpu.SemaphoreType.DMA((2,)),
                pltpu.SemaphoreType.DMA((2,)),
                pltpu.SemaphoreType.DMA((n_slab + 2,)),
                pltpu.SemaphoreType.DMA((3 * n_slab,)),
                pltpu.SemaphoreType.DMA((2, 3, n_slab)),
                pltpu.SemaphoreType.DMA((2, 3, n_slab)),
            ],
            compiler_params=pltpu.CompilerParams(
                collective_id=0, has_side_effects=True, vmem_limit_bytes=48 * 2**20
            ),
        )(
            block_pos.reshape(12),
            features.reshape(12, 64, 512),
            voxel_mask.reshape(12, 64, 8),
            conv_weight.reshape(27, 64, 64),
            conv_gain.reshape(1, -1),
            conv_bias.reshape(1, -1),
            height_weight,
            height_bias.reshape(1, -1),
            bev_weight.reshape(3, -1, chan_out),
            bev_gain.reshape(1, -1),
            bev_bias.reshape(1, -1),
            head_weight,
            head_bias.reshape(1, -1),
        )
        return out.reshape(share, 64, heads)

    in_specs = (
        P(("groups", "strip"), "sub", "slab", None, None, None, None),
        P(("groups", "strip"), "sub", "slab", None, None, None, None),
        P(("groups", "strip"), "sub", "slab", None),
        P(),
        P(),
        P(),
        P("slab", None),
        P(),
        P(),
        P(),
        P(),
        P(),
        P(),
    )
    out_specs = P(("groups", "strip", "slab"), "sub", None)
    return jax.shard_map(
        on_device, mesh=mesh, in_specs=in_specs, out_specs=out_specs, check_vma=False
    )
```

time: 158 us -> 33 us (0.21)
  local copies, waits for them, and re-layouts: 53.4 us -> 6.9 us
  waiting for transfers between devices: 37.4 us -> 0 us
  Pallas kernels: 0 us -> 25.7 us
  matrix products: 23.5 us -> 0 us
  starting transfers between devices: 20.3 us -> 0 us
  between operations: 14.8 us -> 0.12 us
  other arithmetic: 6.64 us -> 0 us
    convert_element_type x6 -> x0, local copies, waits for them, and re-layouts: 36.1 us -> none  [the longest x2 31.5 us: banded_taps(): banded.reshape(3, 3, (edge_len + 2) * chan_count, edge_len * chan_count)]
    pallas_call x0 -> x1, Pallas kernels: none -> 25.7 us  [on_device(): pl.pallas_call(lambda *refs: body((n_strip, n_slab, n_sub), *refs), out_s...]
    unnamed x2 -> x0, waiting for transfers between devices: 25.3 us -> none
    dot_general x29 -> x0, matrix products: 23.5 us -> none  [the longest x18 11.1 us: sweep_taps(): jnp.dot(sliced.reshape(-1, windows.shape[3]), banded[shift_x, shift_y], p...]
    ppermute x10 -> x0, starting transfers between devices: 20.3 us -> none  [the longest x5 13.7 us: extended_2(): lax.ppermute(tail, axis, [(i, (i + 1) % count) for i in range(ends)])]
    ppermute x10 -> x0, waiting for transfers between devices: 12.1 us -> none  [the longest x5 10.7 us: extended_2(): lax.ppermute(head, axis, [((i + 1) % count, i) for i in range(ends)])]
    slice x8 -> x0, local copies, waits for them, and re-layouts: 4.23 us -> none  [the longest x1 3.14 us: sweep_taps(): sliced = windows[:, shift_x:shift_x + rows_x, shift_y:shift_y + rows_y, :]]
    unnamed x30 -> x24, local copies, waits for them, and re-layouts: 2.47 us -> 6.2 us
  transfers between devices with their start and end apart: 11 -> 0, of which waited for: 5 -> 0; matrix products, arithmetic and copies ran while one was open for 32% -> 0% of each run, Pallas kernels for 0% -> 0%
where the time goes in v1:
time: 33 us; the launch traced here: 32.7 us
  Pallas kernels  25.7 us (78%)
  local copies, waits for them, and re-layouts  6.9 us (21%)
    pallas_call x1, Pallas kernels, on_device(): pl.pallas_call(lambda *refs: body((n_strip, n_slab, n_sub), *refs), out_s...  25.7 us
    unnamed x24, local copies, waits for them, and re-layouts  6.2 us
    reshape x1, local copies, waits for them, and re-layouts, on_device(): return out.reshape(share, 64, heads)  0.71 us

profile of v1, /device:TPU:0, one launch (start us, length us, event | category | flops | bytes accessed | tf_op | source)
XLA Modules:
  0.0 32.7 jit_solution(17535513077463759748)
XLA Ops:
  0.0 0.0 copy-start.1
  0.0 0.9 %copy.15.refs_11_ = bf16[256,11]{1,0:T(8,128)(2,1)S(1)} copy(bf16[256,11]{0,1:T(8,128)(2,1)} %param.24) | data formatting | bytes 11264 | tf_op args[11]
  0.9 0.0 copy-start.5
  0.9 0.0 copy-start.7
  0.9 0.0 copy-start.8
  0.9 0.0 copy-start.9
  0.9 0.0 copy-start.10
  1.0 1.6 %copy.14 = s32[1,1,1,12,8,8,8]{6,5,4,3,2,1,0:T(8,128)S(1)} copy(s32[1,1,1,12,8,8,8]{3,6,5,4,2,1,0:T(8,128)} %param.14) | data formatting | bytes 49152 | tf_op args[1]
  2.5 0.0 copy-start.4
  2.5 0.0 copy-start.6
  2.5 0.0 copy-done.1
  2.5 0.0 copy-done.5
  2.5 0.0 copy-done.7
  2.6 0.0 copy-done.8
  2.6 0.0 copy-done.9
  2.6 0.0 copy-done.10
  2.6 0.6 %copy-done.4 = f32[256]{0:T(256)S(1)} copy-done((f32[256]{0:T(256)S(1)}, f32[256]{0:T(256)}, u32[]{:S(2)}) %copy-start.4) | copy-done | bytes 1048
  3.2 0.0 copy-done.6
  3.2 0.0 copy-start
  3.2 1.1 %copy-done = bf16[1,1,1,12,8,8,512]{6,5,4,3,2,1,0:T(8,128)(2,1)S(1)} copy-done((bf16[1,1,1,12,8,8,512]{6,5,4,3,2,1,0:T(8,128)(2,1)S(1)}, bf16[1,1,1,12,8,8,512]{6,5,4,3,2,1,0:T(8,128)(2,1)}, u32[]{:S(2)}) %copy-start) | copy-done | bytes 786456
  4.3 1.0 %copy-done.2 = bf16[3,3,3,64,64]{4,3,2,1,0:T(8,128)(2,1)S(1)} copy-done((bf16[3,3,3,64,64]{4,3,2,1,0:T(8,128)(2,1)S(1)}, bf16[3,3,3,64,64]{4,3,2,1,0:T(8,128)(2,1)}, u32[]{:S(2)}) %copy-start.2) | copy-done | bytes 221208
  5.4 0.9 %copy-done.3 = bf16[1024,128]{1,0:T(8,128)(2,1)S(1)} copy-done((bf16[1024,128]{1,0:T(8,128)(2,1)S(1)}, bf16[1024,128]{1,0:T(8,128)(2,1)}, u32[]{:S(2)}) %copy-start.3) | copy-done | bytes 262168
  6.3 25.7 %shard_map.127 = f32[256,11]{1,0:T(8,128)S(1)} custom-call(s32[12]{0:T(128)S(1)} %bitcast.19, bf16[12,64,512]{2,1,0:T(8,128)(2,1)S(1)} %bitcast.13, s32[12,64,8]{2,1,0:T(8,128)S(1)} %bitcast.12, bf16[27,64,64]{2,1,0:T(8,128)(2,1)S(1)} %bitcast.16, f32[1,64]{1,0:T(1,128)S(1)} %bitcast.20, f32[1,64]{1,0:T(1,128)S(1)} %bitcast.21, ...), custom_call_target="tpu_custom_call" | custom-call | tf_op jit(solution)/shard_map/pallas_call | solution.py:475
  32.0 0.7 %copy.16 = f32[4,64,11]{1,0,2:T(4,128)} copy(f32[4,64,11]{2,1,0:T(8,128)S(1)} %bitcast.15) | data formatting | bytes 22528 | tf_op jit(solution)/shard_map/reshape | solution.py:521
  (2 shorter events, 0.0 us)
Async XLA Ops:
  0.0 2.5 %copy-start.1 = (bf16[3,3,128,256]{3,2,1,0:T(8,128)(2,1)S(1)}, bf16[3,3,128,256]{3,2,1,0:T(8,128)(2,1)}, u32[]{:S(2)}) copy-start(bf16[3,3,128,256]{3,2,1,0:T(8,128)(2,1)} %param.21) | copy-start | bytes 1769476
  0.9 1.6 %copy-start.5 = (f32[256]{0:T(256)S(1)}, f32[256]{0:T(256)}, u32[]{:S(2)}) copy-start(f32[256]{0:T(256)} %param.23) | copy-start | bytes 3076
  0.9 1.6 %copy-start.7 = (f32[64]{0:T(128)S(1)}, f32[64]{0:T(128)}, u32[]{:S(2)}) copy-start(f32[64]{0:T(128)} %param.17) | copy-start | bytes 772
  0.9 1.6 %copy-start.8 = (f32[64]{0:T(128)S(1)}, f32[64]{0:T(128)}, u32[]{:S(2)}) copy-start(f32[64]{0:T(128)} %param.18) | copy-start | bytes 772
  0.9 1.6 %copy-start.9 = (f32[128]{0:T(128)S(1)}, f32[128]{0:T(128)}, u32[]{:S(2)}) copy-start(f32[128]{0:T(128)} %param.20) | copy-start | bytes 1540
  0.9 1.6 %copy-start.10 = (f32[11]{0:T(128)S(1)}, f32[11]{0:T(128)}, u32[]{:S(2)}) copy-start(f32[11]{0:T(128)} %param.25) | copy-start | bytes 136
  2.5 0.7 %copy-start.4 = (f32[256]{0:T(256)S(1)}, f32[256]{0:T(256)}, u32[]{:S(2)}) copy-start(f32[256]{0:T(256)} %param.22) | copy-start | bytes 3076
  2.5 0.7 %copy-start.6 = (s32[1,1,1,12]{3,2,1,0:T(1,128)S(1)}, s32[1,1,1,12]{3,2,1,0:T(1,128)}, u32[]{:S(2)}) copy-start(s32[1,1,1,12]{3,2,1,0:T(1,128)} %param.15) | copy-start | bytes 148
  3.2 1.1 %copy-start = (bf16[1,1,1,12,8,8,512]{6,5,4,3,2,1,0:T(8,128)(2,1)S(1)}, bf16[1,1,1,12,8,8,512]{6,5,4,3,2,1,0:T(8,128)(2,1)}, u32[]{:S(2)}) copy-start(bf16[1,1,1,12,8,8,512]{6,5,4,3,2,1,0:T(8,128)(2,1)} %param.13) | copy-start | bytes 2359300
  4.3 1.0 %copy-start.2 = (bf16[3,3,3,64,64]{4,3,2,1,0:T(8,128)(2,1)S(1)}, bf16[3,3,3,64,64]{4,3,2,1,0:T(8,128)(2,1)}, u32[]{:S(2)}) copy-start(bf16[3,3,3,64,64]{4,3,2,1,0:T(8,128)(2,1)} %param.16) | copy-start | bytes 663556
  5.4 0.9 %copy-start.3 = (bf16[1024,128]{1,0:T(8,128)(2,1)S(1)}, bf16[1024,128]{1,0:T(8,128)(2,1)}, u32[]{:S(2)}) copy-start(bf16[1024,128]{1,0:T(8,128)(2,1)} %refs_6_.1) | copy-start | bytes 786436

commit v2 on v1

v2 whole, which is shorter than its diff:
```python
import jax
import jax.numpy as jnp
from jax import lax
from jax.experimental import pallas as pl
from jax.experimental.pallas import tpu as pltpu
from jax.sharding import PartitionSpec as P

BY_DEV = 8
BZ_DEV = 2
MESH = pl.DeviceIdType.MESH
F32 = jnp.float32
BF16 = jnp.bfloat16

DIRS = [(a, b) for a in (-1, 0, 1) for b in (-1, 0, 1) if (a, b) != (0, 0)]
Y_DIRS = [(0, 0)] + DIRS


def body(
    sizes,
    pos_ref,
    feat_hbm,
    mask_hbm,
    posv_hbm,
    cw_hbm,
    gain_hbm,
    bias_hbm,
    hw_hbm,
    hb_hbm,
    bw_hbm,
    bgain_hbm,
    bbias_hbm,
    head_hbm,
    headb_hbm,
    out_ref,
    feat_ref,
    mask_ref,
    posv_ref,
    cw_ref,
    gain_ref,
    bias_ref,
    hw_ref,
    hb_ref,
    bw_ref,
    bgain_ref,
    bbias_ref,
    head_ref,
    headb_ref,
    xbuf,
    xm,
    xp,
    ybuf,
    wide,
    mbuf,
    band,
    part,
    partb,
    edge,
    rbuf,
    cbuf,
    hcol,
    bexp,
    in_sem,
    face_send,
    face_recv,
    y_send,
    y_recv,
    sum_send,
    sum_recv,
    low_send,
    low_recv,
    high_send,
    high_recv,
    col_send,
    col_recv,
):
    n_strip, n_slab, n_sub = sizes
    share = 8 // n_slab
    s = lax.axis_index("strip")
    l = lax.axis_index("slab")
    u = lax.axis_index("sub")

    fetched = (
        (posv_hbm, posv_ref),
        (mask_hbm, mask_ref),
        (feat_hbm, feat_ref),
        (cw_hbm, cw_ref),
        (gain_hbm, gain_ref),
        (bias_hbm, bias_ref),
        (hw_hbm, hw_ref),
        (hb_hbm, hb_ref),
        (bw_hbm, bw_ref),
        (bgain_hbm, bgain_ref),
        (bbias_hbm, bbias_ref),
        (head_hbm, head_ref),
        (headb_hbm, headb_ref),
    )
    fetches = [
        pltpu.make_async_copy(src, dst, in_sem.at[at]) for at, (src, dst) in enumerate(fetched)
    ]
    for fetch in fetches:
        fetch.start()

    xbuf[0] = jnp.zeros((64, 1280), BF16)
    xbuf[9] = jnp.zeros((64, 1280), BF16)
    xbuf[pl.ds(1, 8), :, pl.ds(0, 128)] = jnp.zeros((8, 64, 128), BF16)
    xbuf[pl.ds(1, 8), :, pl.ds(1152, 128)] = jnp.zeros((8, 64, 128), BF16)
    ybuf[...] = jnp.zeros(ybuf.shape, BF16)
    rbuf[...] = jnp.zeros(rbuf.shape, BF16)
    cbuf[...] = jnp.zeros(cbuf.shape, F32)
    part[...] = jnp.zeros(part.shape, F32)

    barrier = pltpu.get_barrier_semaphore()
    for a in (-1, 0, 1):

        @pl.when((s + a >= 0) & (s + a < n_strip))
        def _():
            for dl in range(n_slab):
                for du in range(n_sub):
                    if a == 0 and dl == 0 and du == 0:
                        continue
                    pl.semaphore_signal(
                        barrier,
                        inc=1,
                        device_id={
                            "strip": s + a,
                            "slab": lax.rem(l + dl, n_slab),
                            "sub": lax.rem(u + du, n_sub),
                        },
                        device_id_type=MESH,
                    )

    level_of = lax.rem(lax.broadcasted_iota(jnp.int32, (512, 512), 0), 8)
    chan_of = lax.broadcasted_iota(jnp.int32, (512, 512), 1) // 64
    spread = (level_of == chan_of).astype(F32).astype(BF16)
    own_col = lax.broadcasted_iota(jnp.int32, (64, 512), 1) // 8
    keep = (own_col == lax.broadcasted_iota(jnp.int32, (64, 512), 0)).astype(F32)
    fetches[0].wait()
    fetches[1].wait()
    places = lax.broadcasted_iota(jnp.int32, (16, 12), 0)
    pick = (places == posv_ref[...]).astype(F32).astype(BF16)
    by_place = lax.dot_general(
        pick,
        mask_ref[...].astype(F32).astype(BF16),
        (((1,), (1,)), ((), ())),
        preferred_element_type=F32,
    )
    rows_of = jnp.concatenate([(by_place[p : p + 1] * keep).astype(BF16) for p in range(16)], axis=0)
    wide[...] = jnp.dot(rows_of, spread, preferred_element_type=F32).reshape(16, 64, 512)

    def slot_at(place):
        slot = jnp.int32(0)
        for t in range(12):
            slot = jnp.where(pos_ref[t] == place, t, slot)
        return slot

    fetches[2].wait()
    for pz in range(BZ_DEV):
        for pair in range(BY_DEV // 2):
            masks, blocks = [], []
            for half in range(2):
                place = (2 * pair + half) * BZ_DEV + pz
                mask = wide[place]
                masks.append(mask.reshape(8, 8, 512))
                blocks.append((feat_ref[slot_at(place)].astype(F32) * mask).reshape(8, 8, 512))
            rows = pl.ds(16 * pair, 16)
            mbuf[:, rows, pl.ds(512 * pz, 512)] = jnp.concatenate(masks, axis=1).astype(BF16)
            xbuf[pl.ds(1, 8), rows, pl.ds(128 + 512 * pz, 512)] = jnp.concatenate(
                blocks, axis=1
            ).astype(BF16)

    strips_near = (s > 0).astype(jnp.int32) + (s < n_strip - 1).astype(jnp.int32) + 1
    pl.semaphore_wait(barrier, strips_near * (n_slab * n_sub) - 1)

    def exists(a, b):
        return (s + a >= 0) & (s + a < n_strip) & (l + b >= 0) & (l + b < n_slab)

    sub_to = (u < n_sub - 1, u > 0)
    sub_from = (u > 0, u < n_sub - 1)

    def ranges(a, b):
        src_x, dst_x = {-1: ((1, 1), (9, 1)), 0: ((1, 8), (1, 8)), 1: ((8, 1), (0, 1))}[a]
        src_z, dst_z = {
            -1: ((128, 128), (1152, 128)),
            0: ((128, 1024), (128, 1024)),
            1: ((1024, 128), (0, 128)),
        }[b]
        return pl.ds(*src_x), pl.ds(*dst_x), pl.ds(*src_z), pl.ds(*dst_z)

    def face_copy(at):
        a, b = DIRS[at]
        src_x, dst_x, src_z, dst_z = ranges(a, b)
        return pltpu.make_async_remote_copy(
            src_ref=xbuf.at[src_x, :, src_z],
            dst_ref=xbuf.at[dst_x, :, dst_z],
            send_sem=face_send.at[at],
            recv_sem=face_recv.at[at],
            device_id={"strip": s + a, "slab": l + b},
            device_id_type=MESH,
        )

    def y_copy(side, at):
        a, b = Y_DIRS[at]
        src_x, dst_x, src_z, dst_z = ranges(a, b)
        return pltpu.make_async_remote_copy(
            src_ref=xbuf.at[src_x, pl.ds(48 if side == 0 else 0, 16), src_z],
            dst_ref=ybuf.at[side, dst_x, :, dst_z],
            send_sem=y_send.at[side, at],
            recv_sem=y_recv.at[side, at],
            device_id={
                "strip": s + a,
                "slab": l + b,
                "sub": u + 1 if side == 0 else u - 1,
            },
            device_id_type=MESH,
        )

    for side in range(2):

        @pl.when(sub_to[side])
        def _():
            y_copy(side, 0).start()

    for at, (a, b) in enumerate(DIRS):

        @pl.when(exists(a, b))
        def _():
            face_copy(at).start()
            for side in range(2):

                @pl.when(sub_to[side])
                def _():
                    y_copy(side, at + 1).start()

    fetches[3].wait()

    def make_band(tap, carry):
        blank = jnp.zeros((64, 64), BF16)
        taps = [cw_ref[3 * tap + k] for k in range(3)]
        for e in range(8):
            cols = [taps[e - o - 1] if 0 <= e - o - 1 <= 2 else blank for o in range(4)]
            band[tap, pl.ds(64 * e, 64), :] = jnp.concatenate(cols, axis=1)
        return carry

    lax.fori_loop(0, 9, make_band, 0)

    for fetch in fetches[4:]:
        fetch.wait()

    for side in range(2):

        @pl.when(sub_from[side])
        def _():
            y_copy(side, 0).wait_recv()

    def shift_rows(x, low, width):
        lanes = pl.ds(low, width)
        rows = xbuf[x, :, lanes].astype(F32)
        row_at = lax.broadcasted_iota(jnp.int32, rows.shape, 0)
        before = ybuf[0, x, :, lanes].astype(F32)[15:16]
        after = ybuf[1, x, :, lanes].astype(F32)[0:1]
        xm[x, :, lanes] = jnp.where(row_at == 0, before, pltpu.roll(rows, 1, 0)).astype(BF16)
        xp[x, :, lanes] = jnp.where(row_at == 63, after, pltpu.roll(rows, 63, 0)).astype(BF16)

    def shift_own(x, carry):
        shift_rows(x, 128, 1024)
        return carry

    lax.fori_loop(1, 9, shift_own, 0)

    gain4 = jnp.concatenate([gain_ref[...]] * 4, axis=1)
    bias4 = jnp.concatenate([bias_ref[...]] * 4, axis=1)

    def conv(j, x, count):
        low = pl.multiple_of(256 * j, 256)
        acc = jnp.zeros((count * 64, 256), F32)
        for dx in range(3):
            for dy, source in enumerate((xm, xbuf, xp)):
                window = source[pl.ds(x + dx, count), :, pl.ds(low, 512)].reshape(count * 64, 512)
                acc = acc + jnp.dot(window, band[3 * dx + dy], preferred_element_type=F32)
        mask = mbuf[pl.ds(x, count), :, pl.ds(low, 256)].reshape(count * 64, 256).astype(F32)
        voxels = (jnp.maximum(acc * gain4 + bias4, 0.0) * mask).astype(BF16)
        sums = jnp.dot(voxels, hw_ref[pl.ds(low, 256), :], preferred_element_type=F32)
        part[pl.ds(x + 1, count)] += sums.reshape(count, 64, 128)

    def conv_inner(j, carry):
        conv(j, 1, 6)
        return carry

    lax.fori_loop(1, 3, conv_inner, 0)

    for at, (a, b) in enumerate(DIRS):

        @pl.when(exists(-a, -b))
        def _():
            face_copy(at).wait_recv()
            for side in range(2):

                @pl.when(sub_from[side])
                def _():
                    y_copy(side, at + 1).wait_recv()

    def shift_ends(at, carry):
        shift_rows(9 * at, 0, 1280)
        return carry

    lax.fori_loop(0, 2, shift_ends, 0)

    def shift_rims(x, carry):
        shift_rows(x, 0, 128)
        shift_rows(x, 1152, 128)
        return carry

    lax.fori_loop(1, 9, shift_rims, 0)

    mine = l // (n_slab // 2)

    def conv_half(half):
        def conv_outer(at, carry):
            conv(3 * at, 4 * half, 4)
            return carry

        def conv_end(j, carry):
            conv(j, 7 * half, 1)
            return carry

        lax.fori_loop(0, 2, conv_outer, 0)
        lax.fori_loop(1, 3, conv_end, 0)
        partb[pl.ds(4 * half, 4)] = part[pl.ds(4 * half + 1, 4)].astype(BF16)

    def sum_copy(target, source):
        return pltpu.make_async_remote_copy(
            src_ref=partb.at[pl.ds(target * share, share)],
            dst_ref=rbuf.at[source, pl.ds(1, share)],
            send_sem=sum_send.at[target],
            recv_sem=sum_recv.at[source],
            device_id={"slab": target},
            device_id_type=MESH,
        )

    def low_copy(target, a, source):
        return pltpu.make_async_remote_copy(
            src_ref=partb.at[pl.ds(7 if a else target * share - 1, 1)],
            dst_ref=rbuf.at[source, pl.ds(0, 1)],
            send_sem=low_send.at[target],
            recv_sem=low_recv.at[source],
            device_id={"strip": s + a, "slab": target},
            device_id_type=MESH,
        )

    def high_copy(target, a, source):
        return pltpu.make_async_remote_copy(
            src_ref=partb.at[pl.ds(0 if a else target * share + share, 1)],
            dst_ref=rbuf.at[source, pl.ds(share + 1, 1)],
            send_sem=high_send.at[target],
            recv_sem=high_recv.at[source],
            device_id={"strip": s + a, "slab": target},
            device_id_type=MESH,
        )

    def col_copy(side, a, target, source):
        return pltpu.make_async_remote_copy(
            src_ref=edge.at[side],
            dst_ref=cbuf.at[side, source, pl.ds(8 * (1 - a), 8)],
            send_sem=col_send.at[side, a + 1, target],
            recv_sem=col_recv.at[side, a + 1, source],
            device_id={
                "strip": s + a,
                "slab": target,
                "sub": u + 1 if side == 0 else u - 1,
            },
            device_id_type=MESH,
        )

    has_up = s < n_strip - 1
    has_down = s > 0
    last = n_slab - 1

    conv_half(1 - mine)
    for t in range(n_slab):

        @pl.when(t // (n_slab // 2) != mine)
        def _():
            sum_copy(t, l).start()

    conv_half(mine)

    edge[0] = part[pl.ds(1, 8), 56:64, :][:, 7, :]
    edge[1] = part[pl.ds(1, 8), 0:8, :][:, 0, :]

    for t in range(n_slab):

        @pl.when((l != t) & (t // (n_slab // 2) == mine))
        def _():
            sum_copy(t, l).start()

        if t > 0:

            @pl.when(l != t)
            def _():
                low_copy(t, 0, l).start()

        if t < last:

            @pl.when(l != t)
            def _():
                high_copy(t, 0, l).start()

    @pl.when(has_up)
    def _():
        low_copy(0, 1, l).start()

    @pl.when(has_down)
    def _():
        high_copy(last, -1, l).start()

    for side in range(2):

        @pl.when(sub_to[side])
        def _():
            for t in range(n_slab):
                col_copy(side, 0, t, l).start()

        @pl.when(sub_to[side] & has_up)
        def _():
            col_copy(side, 1, 0, l).start()

        @pl.when(sub_to[side] & has_down)
        def _():
            col_copy(side, -1, last, l).start()

    for source in range(n_slab):

        @pl.when(l != source)
        def _():
            sum_copy(0, source).wait_recv()

        @pl.when(((l > 0) & (l != source)) | ((l == 0) & has_down))
        def _():
            low_copy(0, 1, source).wait_recv()

        @pl.when(((l < last) & (l != source)) | ((l == last) & has_up))
        def _():
            high_copy(0, -1, source).wait_recv()

        for side in range(2):

            @pl.when(sub_from[side])
            def _():
                col_copy(side, 0, 0, source).wait_recv()

            @pl.when(sub_from[side] & (l == 0) & has_down)
            def _():
                col_copy(side, 1, 0, source).wait_recv()

            @pl.when(sub_from[side] & (l == last) & has_up)
            def _():
                col_copy(side, -1, 0, source).wait_recv()

    hb = hb_ref[...]
    first_x = s * 8 + l * share - 1

    col_x = lax.broadcasted_iota(jnp.int32, (24, 128), 0) + (s * 8 - 8)
    for side in range(2):
        col = cbuf[side, 0]
        for source in range(1, n_slab):
            col = col + cbuf[side, source]
        inside = (col_x >= 0) & (col_x < 8 * n_strip) & sub_from[side]
        hcol[side] = jnp.where(inside, jnp.maximum(col + hb, 0.0), 0.0)

    for i in range(share + 2):
        total = part[l * share + i]
        for source in range(n_slab):
            total = total + rbuf[source, i].astype(F32)
        total = jnp.maximum(total + hb, 0.0)
        if i == 0 or i == share + 1:
            row_ok = (first_x + i >= 0) & (first_x + i < 8 * n_strip)
            total = jnp.where(row_ok, total, 0.0)
        row_at = lax.broadcasted_iota(jnp.int32, total.shape, 0)
        before = hcol[0, pl.ds(7 + l * share + i, 1), :]
        after = hcol[1, pl.ds(7 + l * share + i, 1), :]
        bexp[i, :, pl.ds(0, 128)] = jnp.where(row_at == 0, before, pltpu.roll(total, 1, 0)).astype(
            BF16
        )
        bexp[i, :, pl.ds(128, 128)] = total.astype(BF16)
        bexp[i, :, pl.ds(256, 128)] = jnp.where(row_at == 63, after, pltpu.roll(total, 63, 0)).astype(
            BF16
        )

    pre = jnp.zeros((share * 64, bw_ref.shape[2]), F32)
    for dx in range(3):
        pre = pre + jnp.dot(
            bexp[pl.ds(dx, share)].reshape(share * 64, 384), bw_ref[dx], preferred_element_type=F32
        )
    hidden = jnp.maximum(pre * bgain_ref[...] + bbias_ref[...], 0.0).astype(BF16)
    maps = lax.dot_general(
        head_ref[...], hidden, (((1,), (1,)), ((), ())), preferred_element_type=F32
    )
    maps = maps + jnp.transpose(jnp.broadcast_to(headb_ref[...], (8, headb_ref.shape[1])))[:, 0:1]
    for i in range(share):
        out_ref[:, i, :] = maps[:, 64 * i : 64 * i + 64]

    for at, (a, b) in enumerate(DIRS):

        @pl.when(exists(a, b))
        def _():
            face_copy(at).wait_send()
            for side in range(2):

                @pl.when(sub_to[side])
                def _():
                    y_copy(side, at + 1).wait_send()

    for side in range(2):

        @pl.when(sub_to[side])
        def _():
            y_copy(side, 0).wait_send()
            for t in range(n_slab):
                col_copy(side, 0, t, l).wait_send()

        @pl.when(sub_to[side] & has_up)
        def _():
            col_copy(side, 1, 0, l).wait_send()

        @pl.when(sub_to[side] & has_down)
        def _():
            col_copy(side, -1, last, l).wait_send()

    for t in range(n_slab):

        @pl.when(l != t)
        def _():
            sum_copy(t, l).wait_send()
            if t > 0:
                low_copy(t, 0, l).wait_send()
            if t < last:
                high_copy(t, 0, l).wait_send()

    @pl.when(has_up)
    def _():
        low_copy(0, 1, l).wait_send()

    @pl.when(has_down)
    def _():
        high_copy(last, -1, l).wait_send()


def solution(mesh):
    n_strip, n_slab, n_sub = mesh.shape["strip"], mesh.shape["slab"], mesh.shape["sub"]
    share = 8 // n_slab

    def on_device(
        features,
        voxel_mask,
        block_pos,
        conv_weight,
        conv_gain,
        conv_bias,
        height_weight,
        height_bias,
        bev_weight,
        bev_gain,
        bev_bias,
        head_weight,
        head_bias,
    ):
        heads = head_weight.shape[1]
        chan_out = bev_weight.shape[3]
        vmem = pl.BlockSpec(memory_space=pltpu.VMEM)
        far = pl.BlockSpec(memory_space=pl.ANY)
        places = block_pos.reshape(12)
        operands = (
            features.reshape(12, 64, 512),
            voxel_mask.reshape(12, 8, 8, 8).transpose(1, 2, 3, 0).reshape(512, 12),
            places.reshape(1, 12),
            conv_weight.reshape(27, 64, 64),
            conv_gain.reshape(1, -1),
            conv_bias.reshape(1, -1),
            height_weight,
            height_bias.reshape(1, -1),
            bev_weight.reshape(3, -1, chan_out),
            bev_gain.reshape(1, -1),
            bev_bias.reshape(1, -1),
            head_weight.T,
            head_bias.reshape(1, -1),
        )
        out = pl.pallas_call(
            lambda *refs: body((n_strip, n_slab, n_sub), *refs),
            out_shape=jax.ShapeDtypeStruct((heads, share, 64), F32),
            in_specs=[pl.BlockSpec(memory_space=pltpu.SMEM)] + [far] * 13,
            out_specs=vmem,
            scratch_shapes=[pltpu.VMEM(each.shape, each.dtype) for each in operands]
            + [
                pltpu.VMEM((10, 64, 1280), BF16),
                pltpu.VMEM((10, 64, 1280), BF16),
                pltpu.VMEM((10, 64, 1280), BF16),
                pltpu.VMEM((2, 10, 16, 1280), BF16),
                pltpu.VMEM((16, 64, 512), F32),
                pltpu.VMEM((8, 64, 1024), BF16),
                pltpu.VMEM((9, 512, 256), BF16),
                pltpu.VMEM((10, 64, 128), F32),
                pltpu.VMEM((8, 64, 128), BF16),
                pltpu.VMEM((2, 8, 128), F32),
                pltpu.VMEM((n_slab, share + 2, 64, 128), BF16),
                pltpu.VMEM((2, n_slab, 24, 128), F32),
                pltpu.VMEM((2, 24, 128), F32),
                pltpu.VMEM((share + 2, 64, 384), BF16),
                pltpu.SemaphoreType.DMA((13,)),
                pltpu.SemaphoreType.DMA((8,)),
                pltpu.SemaphoreType.DMA((8,)),
                pltpu.SemaphoreType.DMA((2, 9)),
                pltpu.SemaphoreType.DMA((2, 9)),
            ]
            + [pltpu.SemaphoreType.DMA((n_slab,))] * 6
            + [pltpu.SemaphoreType.DMA((2, 3, n_slab))] * 2,
            compiler_params=pltpu.CompilerParams(
                collective_id=0, has_side_effects=True, vmem_limit_bytes=60 * 2**20
            ),
        )(places, *operands)
        return out.transpose(1, 2, 0)

    in_specs = (
        P(("groups", "strip"), "sub", "slab", None, None, None, None),
        P(("groups", "strip"), "sub", "slab", None, None, None, None),
        P(("groups", "strip"), "sub", "slab", None),
        P(),
        P(),
        P(),
        P("slab", None),
        P(),
        P(),
        P(),
        P(),
        P(),
        P(),
    )
    out_specs = P(("groups", "strip", "slab"), "sub", None)
    return jax.shard_map(
        on_device, mesh=mesh, in_specs=in_specs, out_specs=out_specs, check_vma=False
    )
```

time: 33 us -> 25 us (0.76)
  local copies, waits for them, and re-layouts: 6.9 us -> 1.34 us
  Pallas kernels: 25.7 us -> 23.5 us
    unnamed x24 -> x1, local copies, waits for them, and re-layouts: 6.2 us -> 1.34 us
    pallas_call x1, Pallas kernels: 25.7 us -> 23.5 us  [on_device(): pl.pallas_call(lambda *refs: body((n_strip, n_slab, n_sub), *refs), out_s...]
    reshape x1 -> x0, local copies, waits for them, and re-layouts: 0.71 us -> none  [on_device(): return out.reshape(share, 64, heads)]
where the time goes in v2:
time: 25 us; the launch traced here: 24.8 us
  Pallas kernels  23.5 us (94%)
  local copies, waits for them, and re-layouts  1.34 us (5%)
    pallas_call x1, Pallas kernels, on_device(): pl.pallas_call(lambda *refs: body((n_strip, n_slab, n_sub), *refs), out_s...  23.5 us
    unnamed x1, local copies, waits for them, and re-layouts  1.34 us

profile of v2, /device:TPU:0, one launch (start us, length us, event | category | flops | bytes accessed | tf_op | source)
XLA Modules:
  0.0 24.8 jit_solution(7414572347971423060)
XLA Ops:
  0.0 23.5 %shard_map.127 = f32[11,4,64]{2,1,0:T(4,128)} custom-call(s32[12]{0:T(128)} %bitcast.24, bf16[12,64,512]{2,1,0:T(8,128)(2,1)} %bitcast.18, s32[512,12]{1,0:T(8,128)} %bitcast.21, s32[1,12]{1,0:T(1,128)} %bitcast.25, bf16[27,64,64]{2,1,0:T(8,128)(2,1)} %bitcast.20, f32[1,64]{1,0:T(1,128)} %bitcast.28, f32[1,64]{1,0:T(1,128)} %bitcast.29, ...), custom_call_target="tpu_custom_call" | custom-call | tf_op jit(solution)/shard_map/pallas_call | solution.py:587
  23.5 1.3 %copy.15 = f32[4,64,11]{1,0,2:T(4,128)} copy(f32[4,64,11]{1,0,2:T(4,128)} %bitcast.22) | data formatting | bytes 22528

commit v3 on v2

--- a/solution.py
+++ b/solution.py
@@ -52,8 +52,12 @@
     wide,
     mbuf,
     band,
+    zband,
+    zbuf,
+    zm,
+    zp,
+    accb,
     part,
-    partb,
     edge,
     rbuf,
     cbuf,
@@ -100,12 +104,18 @@
     for fetch in fetches:
         fetch.start()
 
-    xbuf[0] = jnp.zeros((64, 1280), BF16)
-    xbuf[9] = jnp.zeros((64, 1280), BF16)
+    for side in (0, 9, 10, 11):
+        xbuf[side] = jnp.zeros((64, 1280), BF16)
+        xm[side] = jnp.zeros((64, 1280), BF16)
+        xp[side] = jnp.zeros((64, 1280), BF16)
+    for low in (0, 1152):
+        for each in (xm, xp):
+            each[pl.ds(1, 8), :, pl.ds(low, 128)] = jnp.zeros((8, 64, 128), BF16)
     xbuf[pl.ds(1, 8), :, pl.ds(0, 128)] = jnp.zeros((8, 64, 128), BF16)
     xbuf[pl.ds(1, 8), :, pl.ds(1152, 128)] = jnp.zeros((8, 64, 128), BF16)
     ybuf[...] = jnp.zeros(ybuf.shape, BF16)
-    rbuf[...] = jnp.zeros(rbuf.shape, BF16)
+    rbuf[...] = jnp.zeros(rbuf.shape, F32)
+    zbuf[...] = jnp.zeros(zbuf.shape, BF16)
     cbuf[...] = jnp.zeros(cbuf.shape, F32)
     part[...] = jnp.zeros(part.shape, F32)
 
@@ -168,6 +178,42 @@
                 blocks, axis=1
             ).astype(BF16)
 
+    fetches[3].wait()
+
+    def make_band(tap, carry):
+        blank = jnp.zeros((64, 64), BF16)
+        taps = [cw_ref[3 * tap + k] for k in range(3)]
+        for e in range(8):
+            cols = [taps[e - o - 1] if 0 <= e - o - 1 <= 2 else blank for o in range(4)]
+            band[tap, pl.ds(64 * e, 64), :] = jnp.concatenate(cols, axis=1)
+        low = jnp.concatenate([taps[0], blank], axis=1)
+        high = jnp.concatenate([blank, taps[2]], axis=1)
+        empty = jnp.zeros((64, 128), BF16)
+        for e, rim in enumerate((empty, low, high, empty)):
+            zband[tap, pl.ds(64 * e, 64), :] = rim
+        return carry
+
+    lax.fori_loop(0, 9, make_band, 0)
+
+    def conv_own(j, sources):
+        low = pl.multiple_of(256 * j, 256)
+        acc = jnp.zeros((512, 256), F32)
+        for dx in range(3):
+            for dy, source in sources:
+                window = source[pl.ds(dx, 8), :, pl.ds(low, 512)].reshape(512, 512)
+                acc = acc + jnp.dot(window, band[3 * dx + dy], preferred_element_type=F32)
+        return acc.reshape(8, 64, 256)
+
+    def conv_middle(j, carry):
+        accb[j] = conv_own(j, ((1, xbuf),))
+        return carry
+
+    def conv_sides(j, carry):
+        accb[j] += conv_own(j, ((0, xm), (2, xp)))
+        return carry
+
+    lax.fori_loop(0, 2, conv_middle, 0)
+
     strips_near = (s > 0).astype(jnp.int32) + (s < n_strip - 1).astype(jnp.int32) + 1
     pl.semaphore_wait(barrier, strips_near * (n_slab * n_sub) - 1)
 
@@ -189,9 +235,13 @@
     def face_copy(at):
         a, b = DIRS[at]
         src_x, dst_x, src_z, dst_z = ranges(a, b)
+        if b == 0:
+            target = xbuf.at[pl.ds(11 if a < 0 else 10, 1), :, dst_z]
+        else:
+            target = zbuf.at[dst_x, :, pl.ds(128 if b < 0 else 0, 128)]
         return pltpu.make_async_remote_copy(
             src_ref=xbuf.at[src_x, :, src_z],
-            dst_ref=xbuf.at[dst_x, :, dst_z],
+            dst_ref=target,
             send_sem=face_send.at[at],
             recv_sem=face_recv.at[at],
             device_id={"strip": s + a, "slab": l + b},
@@ -231,17 +281,7 @@
                 def _():
                     y_copy(side, at + 1).start()
 
-    fetches[3].wait()
-
-    def make_band(tap, carry):
-        blank = jnp.zeros((64, 64), BF16)
-        taps = [cw_ref[3 * tap + k] for k in range(3)]
-        for e in range(8):
-            cols = [taps[e - o - 1] if 0 <= e - o - 1 <= 2 else blank for o in range(4)]
-            band[tap, pl.ds(64 * e, 64), :] = jnp.concatenate(cols, axis=1)
-        return carry
-
-    lax.fori_loop(0, 9, make_band, 0)
+    lax.fori_loop(2, 4, conv_middle, 0)
 
     for fetch in fetches[4:]:
         fetch.wait()
@@ -270,23 +310,7 @@
     gain4 = jnp.concatenate([gain_ref[...]] * 4, axis=1)
     bias4 = jnp.concatenate([bias_ref[...]] * 4, axis=1)
 
-    def conv(j, x, count):
-        low = pl.multiple_of(256 * j, 256)
-        acc = jnp.zeros((count * 64, 256), F32)
-        for dx in range(3):
-            for dy, source in enumerate((xm, xbuf, xp)):
-                window = source[pl.ds(x + dx, count), :, pl.ds(low, 512)].reshape(count * 64, 512)
-                acc = acc + jnp.dot(window, band[3 * dx + dy], preferred_element_type=F32)
-        mask = mbuf[pl.ds(x, count), :, pl.ds(low, 256)].reshape(count * 64, 256).astype(F32)
-        voxels = (jnp.maximum(acc * gain4 + bias4, 0.0) * mask).astype(BF16)
-        sums = jnp.dot(voxels, hw_ref[pl.ds(low, 256), :], preferred_element_type=F32)
-        part[pl.ds(x + 1, count)] += sums.reshape(count, 64, 128)
-
-    def conv_inner(j, carry):
-        conv(j, 1, 6)
-        return carry
-
-    lax.fori_loop(1, 3, conv_inner, 0)
+    lax.fori_loop(0, 4, conv_sides, 0)
 
     for at, (a, b) in enumerate(DIRS):
 
@@ -299,37 +323,65 @@
                 def _():
                     y_copy(side, at + 1).wait_recv()
 
+    def shifted(rows, before, after):
+        row_at = lax.broadcasted_iota(jnp.int32, rows.shape, 0)
+        up = jnp.where(row_at == 0, before, pltpu.roll(rows, 1, 0)).astype(BF16)
+        down = jnp.where(row_at == 63, after, pltpu.roll(rows, 63, 0)).astype(BF16)
+        return up, down
+
     def shift_ends(at, carry):
-        shift_rows(9 * at, 0, 1280)
+        lanes = pl.ds(128, 1024)
+        xm[10 + at, :, lanes], xp[10 + at, :, lanes] = shifted(
+            xbuf[10 + at, :, lanes].astype(F32),
+            ybuf[0, 9 * at, :, lanes].astype(F32)[15:16],
+            ybuf[1, 9 * at, :, lanes].astype(F32)[0:1],
+        )
         return carry
 
     lax.fori_loop(0, 2, shift_ends, 0)
 
     def shift_rims(x, carry):
-        shift_rows(x, 0, 128)
-        shift_rows(x, 1152, 128)
+        before, after = [
+            jnp.concatenate(
+                [ybuf[side, x, :, pl.ds(low, 128)].astype(F32) for low in (0, 1152)], axis=1
+            )
+            for side in range(2)
+        ]
+        zm[x], zp[x] = shifted(zbuf[x].astype(F32), before[15:16], after[0:1])
         return carry
 
-    lax.fori_loop(1, 9, shift_rims, 0)
+    lax.fori_loop(0, 10, shift_rims, 0)
 
     mine = l // (n_slab // 2)
 
     def conv_half(half):
-        def conv_outer(at, carry):
-            conv(3 * at, 4 * half, 4)
-            return carry
-
-        def conv_end(j, carry):
-            conv(j, 7 * half, 1)
-            return carry
-
-        lax.fori_loop(0, 2, conv_outer, 0)
-        lax.fori_loop(1, 3, conv_end, 0)
-        partb[pl.ds(4 * half, 4)] = part[pl.ds(4 * half + 1, 4)].astype(BF16)
+        beyond = jnp.zeros((256, 256), F32)
+        for dy, source in enumerate((xm, xbuf, xp)):
+            window = jnp.concatenate([source[10 + half, :, pl.ds(256 * j, 512)] for j in range(4)], axis=0)
+            beyond = beyond + jnp.dot(window, band[6 * half + dy], preferred_element_type=F32)
+        accb[:, 7 * half] += beyond.reshape(4, 64, 256)
+        rims = jnp.zeros((256, 128), F32)
+        for dx in range(3):
+            for dy, source in enumerate((zm, zbuf, zp)):
+                window = source[pl.ds(4 * half + dx, 4)].reshape(256, 256)
+                rims = rims + jnp.dot(window, zband[3 * dx + dy], preferred_element_type=F32)
+        lane = lax.broadcasted_iota(jnp.int32, rims.shape, 1)
+        none = jnp.zeros_like(rims)
+        sums = jnp.zeros((256, 128), F32)
+        for j in range(4):
+            acc = accb[j, pl.ds(4 * half, 4)].reshape(256, 256)
+            if j == 0:
+                acc = acc + jnp.concatenate([jnp.where(lane < 64, rims, 0.0), none], axis=1)
+            if j == 3:
+                acc = acc + jnp.concatenate([none, jnp.where(lane < 64, 0.0, rims)], axis=1)
+            mask = mbuf[pl.ds(4 * half, 4), :, pl.ds(256 * j, 256)].reshape(256, 256).astype(F32)
+            voxels = (jnp.maximum(acc * gain4 + bias4, 0.0) * mask).astype(BF16)
+            sums = sums + jnp.dot(voxels, hw_ref[pl.ds(256 * j, 256), :], preferred_element_type=F32)
+        part[pl.ds(4 * half + 1, 4)] = sums.reshape(4, 64, 128)
 
     def sum_copy(target, source):
         return pltpu.make_async_remote_copy(
-            src_ref=partb.at[pl.ds(target * share, share)],
+            src_ref=part.at[pl.ds(target * share + 1, share)],
             dst_ref=rbuf.at[source, pl.ds(1, share)],
             send_sem=sum_send.at[target],
             recv_sem=sum_recv.at[source],
@@ -339,7 +391,7 @@
 
     def low_copy(target, a, source):
         return pltpu.make_async_remote_copy(
-            src_ref=partb.at[pl.ds(7 if a else target * share - 1, 1)],
+            src_ref=part.at[pl.ds(8 if a else target * share, 1)],
             dst_ref=rbuf.at[source, pl.ds(0, 1)],
             send_sem=low_send.at[target],
             recv_sem=low_recv.at[source],
@@ -349,7 +401,7 @@
 
     def high_copy(target, a, source):
         return pltpu.make_async_remote_copy(
-            src_ref=partb.at[pl.ds(0 if a else target * share + share, 1)],
+            src_ref=part.at[pl.ds(1 if a else target * share + share + 1, 1)],
             dst_ref=rbuf.at[source, pl.ds(share + 1, 1)],
             send_sem=high_send.at[target],
             recv_sem=high_recv.at[source],
@@ -470,7 +522,7 @@
     for i in range(share + 2):
         total = part[l * share + i]
         for source in range(n_slab):
-            total = total + rbuf[source, i].astype(F32)
+            total = total + rbuf[source, i]
         total = jnp.maximum(total + hb, 0.0)
         if i == 0 or i == share + 1:
             row_ok = (first_x + i >= 0) & (first_x + i < 8 * n_strip)
@@ -591,17 +643,21 @@
             out_specs=vmem,
             scratch_shapes=[pltpu.VMEM(each.shape, each.dtype) for each in operands]
             + [
-                pltpu.VMEM((10, 64, 1280), BF16),
-                pltpu.VMEM((10, 64, 1280), BF16),
-                pltpu.VMEM((10, 64, 1280), BF16),
+                pltpu.VMEM((12, 64, 1280), BF16),
+                pltpu.VMEM((12, 64, 1280), BF16),
+                pltpu.VMEM((12, 64, 1280), BF16),
                 pltpu.VMEM((2, 10, 16, 1280), BF16),
                 pltpu.VMEM((16, 64, 512), F32),
                 pltpu.VMEM((8, 64, 1024), BF16),
                 pltpu.VMEM((9, 512, 256), BF16),
+                pltpu.VMEM((9, 256, 128), BF16),
+                pltpu.VMEM((10, 64, 256), BF16),
+                pltpu.VMEM((10, 64, 256), BF16),
+                pltpu.VMEM((10, 64, 256), BF16),
+                pltpu.VMEM((4, 8, 64, 256), F32),
                 pltpu.VMEM((10, 64, 128), F32),
-                pltpu.VMEM((8, 64, 128), BF16),
                 pltpu.VMEM((2, 8, 128), F32),
-                pltpu.VMEM((n_slab, share + 2, 64, 128), BF16),
+                pltpu.VMEM((n_slab, share + 2, 64, 128), F32),
                 pltpu.VMEM((2, n_slab, 24, 128), F32),
                 pltpu.VMEM((2, 24, 128), F32),
                 pltpu.VMEM((share + 2, 64, 384), BF16),

time: 25 us -> 23.6 us (0.944)
  Pallas kernels: 23.5 us -> 22 us
    pallas_call x1, Pallas kernels: 23.5 us -> 22 us  [on_device(): pl.pallas_call(lambda *refs: body((n_strip, n_slab, n_sub), *refs), out_s...]
where the time goes in v3:
time: 23.6 us; the launch traced here: 23.4 us
  Pallas kernels  22 us (93%)
  local copies, waits for them, and re-layouts  1.34 us (6%)
    pallas_call x1, Pallas kernels, on_device(): pl.pallas_call(lambda *refs: body((n_strip, n_slab, n_sub), *refs), out_s...  22 us
    unnamed x1, local copies, waits for them, and re-layouts  1.34 us

profile of v3, /device:TPU:0, one launch (start us, length us, event | category | flops | bytes accessed | tf_op | source)
XLA Modules:
  0.0 23.4 jit_solution(9763931065622972960)
XLA Ops:
  0.0 22.0 %shard_map.127 = f32[11,4,64]{2,1,0:T(4,128)} custom-call(s32[12]{0:T(128)} %bitcast.24, bf16[12,64,512]{2,1,0:T(8,128)(2,1)} %bitcast.18, s32[512,12]{1,0:T(8,128)} %bitcast.21, s32[1,12]{1,0:T(1,128)} %bitcast.25, bf16[27,64,64]{2,1,0:T(8,128)(2,1)} %bitcast.20, f32[1,64]{1,0:T(1,128)} %bitcast.28, f32[1,64]{1,0:T(1,128)} %bitcast.29, ...), custom_call_target="tpu_custom_call" | custom-call | tf_op jit(solution)/shard_map/pallas_call | solution.py:639
  22.1 1.3 %copy.15 = f32[4,64,11]{1,0,2:T(4,128)} copy(f32[4,64,11]{1,0,2:T(4,128)} %bitcast.22) | data formatting | bytes 22528

commit v4 on v3

--- a/solution.py
+++ b/solution.py
@@ -101,7 +101,7 @@
     fetches = [
         pltpu.make_async_copy(src, dst, in_sem.at[at]) for at, (src, dst) in enumerate(fetched)
     ]
-    for fetch in fetches:
+    for fetch in fetches[:4]:
         fetch.start()
 
     for side in (0, 9, 10, 11):
@@ -164,6 +164,8 @@
         return slot
 
     fetches[2].wait()
+    for fetch in fetches[4:]:
+        fetch.start()
     for pz in range(BZ_DEV):
         for pair in range(BY_DEV // 2):
             masks, blocks = [], []
@@ -197,11 +199,16 @@
 
     def conv_own(j, sources):
         low = pl.multiple_of(256 * j, 256)
-        acc = jnp.zeros((512, 256), F32)
-        for dx in range(3):
-            for dy, source in sources:
-                window = source[pl.ds(dx, 8), :, pl.ds(low, 512)].reshape(512, 512)
-                acc = acc + jnp.dot(window, band[3 * dx + dy], preferred_element_type=F32)
+        taps = [(dx, dy, source) for dx in range(3) for dy, source in sources]
+        windows = [
+            source[pl.ds(dx, 8), :, pl.ds(low, 512)].reshape(512, 512) for dx, dy, source in taps
+        ]
+        weights = [band[3 * dx + dy] for dx, dy, source in taps]
+        acc = jnp.dot(
+            jnp.concatenate(windows, axis=1),
+            jnp.concatenate(weights, axis=0),
+            preferred_element_type=F32,
+        )
         return acc.reshape(8, 64, 256)
 
     def conv_middle(j, carry):

time: 23.6 us -> 23.6 us (level)
  no operation moved by 1% of the time
where the time goes in v4:
time: 23.6 us; the launch traced here: 23.4 us
  Pallas kernels  22 us (93%)
  local copies, waits for them, and re-layouts  1.34 us (6%)
    pallas_call x1, Pallas kernels, on_device(): pl.pallas_call(lambda *refs: body((n_strip, n_slab, n_sub), *refs), out_s...  22 us
    unnamed x1, local copies, waits for them, and re-layouts  1.34 us

profile of v4, /device:TPU:0, one launch (start us, length us, event | category | flops | bytes accessed | tf_op | source)
XLA Modules:
  0.0 23.4 jit_solution(1223537394131288758)
XLA Ops:
  0.0 22.0 %shard_map.127 = f32[11,4,64]{2,1,0:T(4,128)} custom-call(s32[12]{0:T(128)} %bitcast.24, bf16[12,64,512]{2,1,0:T(8,128)(2,1)} %bitcast.18, s32[512,12]{1,0:T(8,128)} %bitcast.21, s32[1,12]{1,0:T(1,128)} %bitcast.25, bf16[27,64,64]{2,1,0:T(8,128)(2,1)} %bitcast.20, f32[1,64]{1,0:T(1,128)} %bitcast.28, f32[1,64]{1,0:T(1,128)} %bitcast.29, ...), custom_call_target="tpu_custom_call" | custom-call | tf_op jit(solution)/shard_map/pallas_call | solution.py:646
  22.1 1.3 %copy.15 = f32[4,64,11]{1,0,2:T(4,128)} copy(f32[4,64,11]{1,0,2:T(4,128)} %bitcast.22) | data formatting | bytes 22528
